TPU v7x, 32 devices: a whole 2x2x4 slice. The times are simulated.
32 devices in a mesh: groups: 2 (over y), bead: 4 (over z), space: 4 (over x, core).
Axes of the slice: x: 2, y: 2, z: 4, core: 2. Of those that a mesh axis runs over, the one named last changes fastest.
Arguments:
- positions: float32 [8, 3, 96, 128], P(('groups', 'bead'), None, 'space'), parts along dimension 0, may hold values from -5 to 5
- momenta: float32 [8, 3, 96, 128], P(('groups', 'bead'), None, 'space'), parts along dimension 0, may hold values from -6 to 6
- forces: float32 [8, 3, 96, 128], P(('groups', 'bead'), None, 'space'), parts along dimension 0, may hold values from -6 to 6
- noise: float32 [8, 3, 96, 128], P(('groups', 'bead'), None, 'space'), parts along dimension 0, may hold values from -5 to 5
- masses: float32 [192, 128], P(('groups', 'space')), parts along dimension 0, may hold values from 1 to 16
- strengths: float32 [192, 128], P(('groups', 'space')), parts along dimension 0, may hold values from 0.5 to 2
- cell_counts: int32 [192], P('groups'), parts along dimension 0, may hold values from 32 to 128, as said below
- neighbour_cells: int32 [192, 26], P(('groups', 'space')), parts along dimension 0, may hold values from -1 to 95, as said below
Outputs:
- positions_next: float32 [8, 3, 96, 128], P(('groups', 'bead'), None, 'space'), parts along dimension 0
- momenta_next: float32 [8, 3, 96, 128], P(('groups', 'bead'), None, 'space'), parts along dimension 0
- forces_next: float32 [8, 3, 96, 128], P(('groups', 'bead'), None, 'space'), parts along dimension 0
There are 2 independent parts, one for each index of `groups`. A program takes and returns all parts, laid end to end along the dimension named above; each array names one. Nothing has to cross between parts.
Inputs may be any that keep to these rules, and one draw needn't show every extreme that they name: `neighbour_cells`: row c lists 26 different cells c + d with 0 < |d| <= 16, always c - 1 and c + 1 among them; an entry is -1 where c + d lies outside the system's cells. `cell_counts`: A cell's atoms fill its first slots; some cell of each system is full.
All inputs are finite; a program needn't handle non-finite values.
Results may differ from a plain program's by a relative error of at most 0.0003.
Values sent between devices are 32-bit elements; how exact they have to be, the bound alone decides.
A program may use at most 64 MiB of HBM per device.

v0:
```python
import jax
import jax.numpy as jnp
from jax import lax
from jax.sharding import PartitionSpec as P

HALO = 16


TIME_STEP = 0.5
CYCLE_FREQ = 1.5
GAMMA_ZERO = 0.5
PAIR_SCALE = 0.005


def extended(block, sides, width):
    for axis, dim in sides:
        count = lax.axis_size(axis)
        forward = [(i, i + 1) for i in range(count - 1)]
        backward = [(target, source) for source, target in forward]
        low = lax.ppermute(
            lax.slice_in_dim(block, block.shape[dim] - width, None, axis=dim), axis, forward
        )
        high = lax.ppermute(lax.slice_in_dim(block, 0, width, axis=dim), axis, backward)
        block = jnp.concatenate([low, block, high], axis=dim)
    return block


def modes_table(beads):
    rowsk = jnp.arange(beads, dtype=jnp.int32)[:, None]
    colsj = jnp.arange(beads, dtype=jnp.int32)[None, :]
    angle = 2.0 * jnp.pi * (rowsk * colsj % beads).astype(jnp.float32) / beads
    parity = jnp.where(colsj % 2 == 0, 1.0, -1.0).astype(jnp.float32)
    factor = jnp.sqrt(2.0 / beads)
    plain = jnp.ones_like(angle) / jnp.sqrt(1.0 * beads)
    table = jnp.where(
        rowsk == 0,
        plain,
        jnp.where(
            rowsk < beads // 2,
            factor * jnp.cos(angle),
            jnp.where(rowsk == beads // 2, parity * plain, factor * jnp.sin(angle)),
        ),
    )
    return table


def evolve(coords, moment, modeval, masses_here, kicks, beads):
    freq = 2.0 * CYCLE_FREQ * jnp.sin(jnp.pi * modeval / beads)
    half_step = 0.25 * TIME_STEP * 2.0
    centroid = modeval == 0.0
    cosine = jnp.cos(freq * half_step)
    sine_part = jnp.sin(freq * half_step)
    reach_term = jnp.where(centroid, half_step, sine_part / jnp.where(centroid, 1.0, freq))

    def rotate(coord_in, moment_in):
        return (
            cosine * coord_in + reach_term / masses_here * moment_in,
            -masses_here * freq * sine_part * coord_in + cosine * moment_in,
        )

    coords, moment = rotate(coords, moment)
    damping = jnp.exp(-jnp.where(centroid, GAMMA_ZERO, 2.0 * freq) * TIME_STEP)
    moment = damping * moment + jnp.sqrt(1.0 - damping * damping) * jnp.sqrt(masses_here) * kicks
    return rotate(coords, moment)


def cell_force(own_coords, own_weight, far_coords, far_weight):
    distance = jnp.sum((own_coords[:, :, None, None] - far_coords[:, None, :, :]) ** 2, axis=0)
    kernel = (
        PAIR_SCALE * own_weight[:, None, None] * far_weight[None, :, :] * jnp.exp(-0.5 * distance)
    )
    total = jnp.sum(kernel, axis=(1, 2))
    slots = own_coords.shape[1]
    pulled = jnp.dot(
        kernel.reshape(slots, -1), far_coords.reshape(3, -1).T, precision=lax.Precision.HIGHEST
    )
    return own_coords * total[None, :] - pulled.T


def per_device(positions, momenta, forces, noise, masses, strengths, cell_counts, neighbour_cells):
    beads = lax.axis_size("bead")
    bead_index = lax.axis_index("bead")
    space_index = lax.axis_index("space")
    ncells = positions.shape[2]
    slots = positions.shape[3]
    table = modes_table(beads)
    column = lax.dynamic_index_in_dim(table, bead_index, 1, keepdims=False)
    moment_half = momenta + 0.25 * forces
    stacked = jnp.concatenate([positions, moment_half], axis=1)[0]
    coeff = column
    mine = lax.psum_scatter(
        (coeff[:, None, None, None] * stacked[None]).reshape(
            6 * lax.axis_size("bead"), ncells, slots
        ),
        "bead",
        scatter_dimension=0,
        tiled=True,
    )
    modeval = bead_index.astype(jnp.float32)
    new_coords, new_moment = evolve(mine[0:3], mine[3:6], modeval, masses, noise[0], beads)
    mode_pair = jnp.concatenate([new_coords, new_moment], axis=0)[None]
    coeff = column
    stacked = jnp.einsum(
        "j,jxcs->xcs",
        coeff,
        lax.all_gather(mode_pair, "bead", axis=0, tiled=True),
        precision=lax.Precision.HIGHEST,
    )
    coords = stacked[0:3]
    moved_moment = stacked[3:6]
    own_counts = lax.dynamic_slice_in_dim(cell_counts, space_index * ncells, ncells)
    live = (jnp.arange(slots, dtype=jnp.int32)[None, :] < own_counts[:, None]).astype(jnp.float32)
    weights = strengths * live
    packed = jnp.concatenate([coords, weights[None]], axis=0)
    widened = extended(packed, (("space", 1),), HALO)
    local_list = jnp.where(neighbour_cells >= 0, neighbour_cells - space_index * ncells + HALO, -1)
    partners = jnp.concatenate(
        [jnp.arange(ncells, dtype=jnp.int32)[:, None] + HALO, local_list], axis=1
    )

    def one_cell(pair):
        cell_index, plist = pair
        usable = (plist >= 0).astype(jnp.float32)
        index_list = jnp.maximum(plist, 0)
        gathered = widened[:, index_list]
        far_weight = gathered[3] * usable[:, None]
        return cell_force(coords[:, cell_index], weights[cell_index], gathered[0:3], far_weight)

    result = lax.map(one_cell, (jnp.arange(ncells, dtype=jnp.int32), partners))
    forces_next = jnp.transpose(result, (1, 0, 2))
    momenta_next = moved_moment + 0.25 * forces_next
    return (coords[None], momenta_next[None], forces_next[None])


def solution(mesh):
    in_specs = (
        P(("groups", "bead"), None, "space", None),
        P(("groups", "bead"), None, "space", None),
        P(("groups", "bead"), None, "space", None),
        P(("groups", "bead"), None, "space", None),
        P(("groups", "space"), None),
        P(("groups", "space"), None),
        P("groups"),
        P(("groups", "space"), None),
    )
    out_specs = (
        P(("groups", "bead"), None, "space", None),
        P(("groups", "bead"), None, "space", None),
        P(("groups", "bead"), None, "space", None),
    )
    return jax.shard_map(
        per_device, mesh=mesh, in_specs=in_specs, out_specs=out_specs, check_vma=False
    )
```

profile of v0, /device:TPU:1, one launch (start us, length us, event | category | flops | bytes accessed | tf_op | source)
XLA Modules:
  0.0 213.3 jit_solution(8675016851745885721)
XLA Ops:
  14.0 16.6 %reduce-scatter.2.cloned.1.call-done = f32[6,24,128]{2,1,0:T(8,128)} async-done(((f32[24,24,128]{2,1,0:T(8,128)}), f32[6,24,128]{2,1,0:T(8,128)}) %reduce-scatter.2.cloned.1.call-update) | async-done | bytes 73744 | tf_op jit(solution)/shard_map/reduce_scatter | solution.py:91
  32.3 11.4 %all-gather = f32[24,24,128]{2,1,0:T(8,128)S(1)} all-gather(f32[6,24,128]{2,1,0:T(8,128)S(1)} %pad_maximum_fusion.1), channel_id=2, replica_groups=mesh['groups'=2,'bead'=4,'space'=4] {'bead'}, dimensions={0}, use_global_device_ids=true | all-gather | bytes 368640 | tf_op jit(solution)/shard_map/all_gather | solution.py:106
  44.3 7.9 %collective-permute-start = (f32[4,16,128]{2,1,0:T(8,128)S(1)}, f32[4,16,128]{2,1,0:T(8,128)S(1)}, u32[]{:S(2)}, u32[]{:S(2)}) collective-permute-start(f32[4,16,128]{2,1,0:T(8,128)S(1)} %get-tuple-element.87), channel_id=1, source_target_pairs={{0,1},{1,2},{2,3},{4,5},{5,6},{6,7},{8,9},{9,10},{10,11},{12,13},{... | collective-permute-start | bytes 98312 | tf_op jit(solution)/shard_map/ppermute | solution.py:20
  52.3 1.9 collective-permute-start.1
  54.3 3.2 %collective-permute-done.1 = f32[4,16,128]{2,1,0:T(8,128)S(1)} collective-permute-done((f32[4,16,128]{2,1,0:T(8,128)S(1)}, f32[4,16,128]{2,1,0:T(8,128)S(1)}, u32[]{:S(2)}, u32[]{:S(2)}) %collective-permute-start.1) | collective-permute-done | bytes 32800 | tf_op jit(solution)/shard_map/ppermute | solution.py:23
  57.5 148.2 %while.10 = (s32[]{:T(128)}, f32[24,3,128]{2,0,1:T(8,128)S(1)}, s32[24]{0:T(128)S(1)}, f32[3,24,128]{2,1,0:T(8,128)S(1)}, f32[24,128]{1,0:T(8,128)S(1)}, /*index...) while((s32[]{:T(128)}, f32[24,3,128]{2,0,1:T(8,128)S(1)}, ...), condition=%wide.region_4.5_spmd, body=%wide.region_1.4_spmd.sunk | while | flops 22566100 | bytes 5706651 | solution.py:129
  62.1 1.6 fusion.36
  68.2 1.6 fusion.36
  74.4 1.6 fusion.36
  80.6 1.6 fusion.36
  86.8 1.6 fusion.36
  93.0 1.6 fusion.36
  99.1 1.6 fusion.36
  105.3 1.6 fusion.36
  111.5 1.6 fusion.36
  117.7 1.6 fusion.36
  123.8 1.6 fusion.36
  130.0 1.6 fusion.36
  136.2 1.6 fusion.36
  142.4 1.6 fusion.36
  148.6 1.6 fusion.36
  154.7 1.6 fusion.36
  185.6 1.6 fusion.36
  191.8 1.6 fusion.36
  (399 shorter events, 80.0 us)
Async XLA Ops:
  7.2 23.5 %reduce-scatter.2.cloned.1.call-start = ((), (), s32[]{:S(2)}) async-start(), calls=%async_computation.1 | async-start | bytes 368640 | tf_op jit(solution)/shard_map/reduce_scatter | solution.py:91
  44.3 9.9 %collective-permute-start = (f32[4,16,128]{2,1,0:T(8,128)S(1)}, f32[4,16,128]{2,1,0:T(8,128)S(1)}, u32[]{:S(2)}, u32[]{:S(2)}) collective-permute-start(f32[4,16,128]{2,1,0:T(8,128)S(1)} %get-tuple-element.87), channel_id=1, source_target_pairs={{0,1},{1,2},{2,3},{4,5},{5,6},{6,7},{8,9},{9,10},{10,11},{12,13},{... | collective-permute-start | bytes 98312 | tf_op jit(solution)/shard_map/ppermute | solution.py:20
  52.3 5.2 %collective-permute-start.1 = (f32[4,16,128]{2,1,0:T(8,128)S(1)}, f32[4,16,128]{2,1,0:T(8,128)S(1)}, u32[]{:S(2)}, u32[]{:S(2)}) collective-permute-start(f32[4,16,128]{2,1,0:T(8,128)S(1)} %get-tuple-element.88), channel_id=1, source_target_pairs={{1,0},{2,1},{3,2},{5,4},{6,5},{7,6},{9,8},{10,9},{11,10},{13,12},{... | collective-permute-start | bytes 98312 | tf_op jit(solution)/shard_map/ppermute | solution.py:23
  205.8 0.7 copy-start
Sparse Core Ops, SparseCore 0:
  10.3 20.2 reduce-scatter.1
where the time goes:
time: 215 us; the launch traced here: 213 us
  loops' own time  49 us (23%)
  matrix products  39 us (18%)
  other arithmetic  38.6 us (18%)
  local copies, waits for them, and re-layouts  31 us (14%)
  waiting for transfers between devices  19.8 us (9%)
  between operations  14.5 us (7%)
  blocking collectives  11.4 us (5%)
  starting transfers between devices  9.89 us (5%)
    another operation x1, loops' own time, per_device(): result = lax.map(one_cell, (jnp.arange(ncells, dtype=jnp.int32), partners))  49 us
    dot_general x24, matrix products, cell_force(): jnp.dot(kernel.reshape(slots, -1), far_coords.reshape(3, -1).T, precision...  38.4 us
    reduce_scatter x1, waiting for transfers between devices, per_device(): lax.psum_scatter((coeff[:, None, None, None] * stacked[None]).reshape(6 *...  16.6 us
    reduce_sum x24, other arithmetic, cell_force(): jnp.sum((own_coords[:, :, None, None] - far_coords[:, None, :, :]) ** 2,...  16.2 us
    gather x24, local copies, waits for them, and re-layouts, one_cell(): gathered = widened[:, index_list]  14.5 us
    dynamic_slice x24, local copies, waits for them, and re-layouts, per_device(): result = lax.map(one_cell, (jnp.arange(ncells, dtype=jnp.int32), partners))  14.1 us
    all_gather x1, blocking collectives, per_device(): lax.all_gather(mode_pair, 'bead', axis=0, tiled=True)  11.4 us
    reduce_sum x24, other arithmetic, cell_force(): total = jnp.sum(kernel, axis=(1, 2))  11.3 us
  transfers between devices with their start and end apart: 3, of which 2 were waited for; matrix products, arithmetic and copies ran while one was open for 2% of the time, Pallas kernels for 0%

commit v1 on v0

v1 whole, which is shorter than its diff:
```python
import functools
import math

import jax
import jax.numpy as jnp
import numpy as np
from jax import lax
from jax.experimental import pallas as pl
from jax.experimental.pallas import tpu as pltpu
from jax.sharding import PartitionSpec as P

HALO = 16
TIME_STEP = 0.5
CYCLE_FREQ = 1.5
GAMMA_ZERO = 0.5
PAIR_SCALE = 0.005
ROOT = math.sqrt(math.log2(math.e))
MESH = pl.DeviceIdType.MESH


def modes_table(beads):
    k = np.arange(beads)[:, None]
    j = np.arange(beads)[None, :]
    angle = 2.0 * np.pi * (k * j % beads) / beads
    parity = np.where(j % 2 == 0, 1.0, -1.0)
    plain = np.ones_like(angle) / np.sqrt(beads)
    factor = np.sqrt(2.0 / beads)
    return np.where(
        k == 0,
        plain,
        np.where(
            k < beads // 2,
            factor * np.cos(angle),
            np.where(k == beads // 2, parity * plain, factor * np.sin(angle)),
        ),
    )


def propagator(beads):
    table = modes_table(beads)
    k = np.arange(beads)
    freq = 2.0 * CYCLE_FREQ * np.sin(np.pi * k / beads)
    half = 0.5 * TIME_STEP
    cos, sin = np.cos(freq * half), np.sin(freq * half)
    reach = np.where(k == 0, half, sin / np.where(k == 0, 1.0, freq))
    damp = np.exp(-np.where(k == 0, GAMMA_ZERO, 2.0 * freq) * TIME_STEP)
    kick = np.sqrt(1.0 - damp * damp)
    pull = -freq * sin
    modes = {
        "qq": cos * cos + reach * damp * pull,
        "qp": reach * cos * (1.0 + damp),
        "pq": pull * cos * (1.0 + damp),
        "pp": pull * reach + cos * cos * damp,
    }
    by_offset = {
        name: [float(np.sum(value * table[:, 0] * table[:, d])) for d in range(beads)]
        for name, value in modes.items()
    }
    noise = np.stack([(reach * kick)[:, None] * table, (cos * kick)[:, None] * table])
    return by_offset, noise.astype(np.float32)


def split3(value):
    high = value.astype(jnp.bfloat16).astype(jnp.float32)
    rest = value - high
    mid = rest.astype(jnp.bfloat16).astype(jnp.float32)
    return high, mid, rest - mid


def kernel(
    beads,
    spaces,
    coef,
    kicks_ref,
    counts_ref,
    list_ref,
    pos_ref,
    mom_ref,
    frc_ref,
    noi_ref,
    mass_ref,
    str_ref,
    pos_out,
    mom_out,
    frc_out,
    send_q,
    send_p,
    recv_q,
    recv_p,
    own_r,
    own_w,
    low_r,
    low_w,
    high_r,
    high_w,
    rows_v,
    rows_u,
    rows_w,
    far_b,
    far_r,
    rows_f,
    sq_sem,
    rq_sem,
    sp_sem,
    rp_sem,
    halo_send,
    halo_recv,
):
    bead = lax.axis_index("bead")
    space = lax.axis_index("space")
    cells, slots = mass_ref.shape
    neigh = list_ref.shape[1]
    wide = cells + 2 * HALO
    has_low = space > 0
    has_high = space < spaces - 1

    barrier = pltpu.get_barrier_semaphore()
    for d in range(1, beads):
        pl.semaphore_signal(
            barrier, inc=1, device_id={"bead": lax.rem(bead + d, beads)}, device_id_type=MESH
        )

    @pl.when(has_low)
    def _():
        pl.semaphore_signal(barrier, inc=1, device_id={"space": space - 1}, device_id_type=MESH)

    @pl.when(has_high)
    def _():
        pl.semaphore_signal(barrier, inc=1, device_id={"space": space + 1}, device_id_type=MESH)

    mass = mass_ref[...][None]
    root_mass = jnp.sqrt(mass)
    q = pos_ref[...]
    p = mom_ref[...] + 0.25 * frc_ref[...]
    scaled_p = p / mass
    noise_q = noi_ref[...] / root_mass
    for d in range(beads):
        target = lax.rem(bead + d, beads)
        send_q[d] = coef["qq"][d] * q + coef["qp"][d] * scaled_p + kicks_ref[0, bead, target] * noise_q

    lane = lax.broadcasted_iota(jnp.int32, (1, slots), 1)
    for c in range(cells):
        count = counts_ref[space * cells + c]
        own_w[c : c + 1, :] = jnp.where(lane < count, str_ref[c : c + 1, :], 0.0)

    pl.semaphore_wait(
        barrier, beads - 1 + has_low.astype(jnp.int32) + has_high.astype(jnp.int32)
    )

    def bead_copy(source, target, send, recv, d):
        return pltpu.make_async_remote_copy(
            src_ref=source.at[d],
            dst_ref=target.at[d],
            send_sem=send.at[d],
            recv_sem=recv.at[d],
            device_id={"bead": lax.rem(bead + d, beads)},
            device_id_type=MESH,
        )

    def space_copy(source, target, index, peer):
        return pltpu.make_async_remote_copy(
            src_ref=source,
            dst_ref=target,
            send_sem=halo_send.at[index],
            recv_sem=halo_recv.at[index],
            device_id={"space": peer},
            device_id_type=MESH,
        )

    first = pl.ds(0, HALO)
    last = pl.ds(cells - HALO, HALO)
    up_w = space_copy(own_w.at[last], low_w, 0, space + 1)
    down_w = space_copy(own_w.at[first], high_w, 1, space - 1)
    up_r = space_copy(own_r.at[:, last], low_r, 2, space + 1)
    down_r = space_copy(own_r.at[:, first], high_r, 3, space - 1)
    copies_q = [bead_copy(send_q, recv_q, sq_sem, rq_sem, d) for d in range(1, beads)]
    copies_p = [bead_copy(send_p, recv_p, sp_sem, rp_sem, d) for d in range(1, beads)]
    for copy in copies_q:
        copy.start()

    @pl.when(has_high)
    def _():
        up_w.start()

    @pl.when(has_low)
    def _():
        down_w.start()

    mass_q = mass * q
    noise_p = noi_ref[...] * root_mass
    for d in range(beads):
        target = lax.rem(bead + d, beads)
        send_p[d] = coef["pq"][d] * mass_q + coef["pp"][d] * p + kicks_ref[1, bead, target] * noise_p
    for copy in copies_p:
        copy.start()

    @pl.when(jnp.logical_not(has_low))
    def _():
        low_r[...] = jnp.zeros_like(low_r)
        low_w[...] = jnp.zeros_like(low_w)

    @pl.when(jnp.logical_not(has_high))
    def _():
        high_r[...] = jnp.zeros_like(high_r)
        high_w[...] = jnp.zeros_like(high_w)

    rows_v[...] = jnp.zeros_like(rows_v)
    rows_u[...] = jnp.zeros_like(rows_u)
    rows_w[...] = jnp.zeros_like(rows_w)
    far_b[wide] = jnp.zeros(far_b.shape[1:], far_b.dtype)
    far_r[wide] = jnp.zeros(far_r.shape[1:], far_r.dtype)

    for copy in copies_q:
        copy.wait_recv()
    total = send_q[0]
    for d in range(1, beads):
        total = total + recv_q[d]
    own_r[...] = total
    pos_out[...] = total

    @pl.when(has_high)
    def _():
        up_r.start()

    @pl.when(has_low)
    def _():
        down_r.start()

    def place(start, size, coords, weights):
        scaled = ROOT * coords
        norm = -0.5 * (scaled[0] * scaled[0] + scaled[1] * scaled[1] + scaled[2] * scaled[2])
        region = pl.ds(start, size)
        for x in range(3):
            rows_v[region, x, :] = scaled[x]
            rows_w[region, x, :] = scaled[x] * weights
        rows_v[region, 3, :] = norm
        rows_v[region, 4, :] = jnp.ones_like(norm)
        rows_w[region, 3, :] = weights
        return scaled, norm

    def features(start, size):
        for c in range(start, start + size, 8):
            group = pl.ds(c, 8)
            high, mid, low = split3(rows_v[group])
            far_b[group] = jnp.concatenate([high, high, mid, high, low, mid], axis=1).astype(
                jnp.bfloat16
            )
            value = rows_w[group]
            high = value.astype(jnp.bfloat16).astype(jnp.float32)
            far_r[group] = jnp.concatenate([high, value - high], axis=1).astype(jnp.bfloat16)

    scaled, norm = place(HALO, cells, total, own_w[...])
    for x in range(3):
        rows_u[:, x, :] = scaled[x]
    rows_u[:, 3, :] = jnp.ones_like(norm)
    rows_u[:, 4, :] = norm
    features(HALO, cells)

    @pl.when(has_low)
    def _():
        up_w.wait_recv()
        up_r.wait_recv()

    @pl.when(has_high)
    def _():
        down_w.wait_recv()
        down_r.wait_recv()

    place(0, HALO, low_r[...], low_w[...])
    features(0, HALO)
    place(HALO + cells, HALO, high_r[...], high_w[...])
    features(HALO + cells, HALO)

    def one_cell(c, carry):
        own = rows_u[c]
        high, mid, low = split3(own)
        stacked = jnp.concatenate([high, mid, high, low, high, mid], axis=0)
        stacked = jnp.concatenate(
            [stacked, jnp.zeros((slots - stacked.shape[0], slots), jnp.float32)], axis=0
        )
        left = jnp.transpose(stacked)[:, :48].astype(jnp.bfloat16)
        partners = [c + HALO]
        for n in range(neigh):
            entry = list_ref[c, n]
            local = jnp.clip(entry - space * cells + HALO, 0, wide - 1)
            partners.append(jnp.where(entry >= 0, local, wide))
        if len(partners) % 2:
            partners.append(wide)
        acc = jnp.zeros((16, slots), jnp.float32)
        for n in range(0, len(partners), 2):
            one, two = partners[n], partners[n + 1]
            right = jnp.concatenate([far_b[one], far_b[two]], axis=1)
            power = lax.dot_general(
                left, right, (((1,), (0,)), ((), ())), preferred_element_type=jnp.float32
            )
            value = jnp.exp2(power)
            near = value.astype(jnp.bfloat16)
            rest = (value - near.astype(jnp.float32)).astype(jnp.bfloat16)
            pulls = jnp.concatenate([far_r[one], far_r[two]], axis=1)
            contract = (((1,), (1,)), ((), ()))
            acc = acc + lax.dot_general(pulls, near, contract, preferred_element_type=jnp.float32)
            acc = acc + lax.dot_general(pulls, rest, contract, preferred_element_type=jnp.float32)
        sums = acc[0:8] + acc[8:16]
        weight = rows_w[c + HALO][3:4]
        rows_f[c] = (PAIR_SCALE / ROOT) * weight * (own * sums[3:4] - sums)
        return carry

    lax.fori_loop(0, cells, one_cell, 0)

    for copy in copies_p:
        copy.wait_recv()
    moved = send_p[0]
    for d in range(1, beads):
        moved = moved + recv_p[d]
    for x in range(3):
        force = rows_f[:, x, :]
        frc_out[x] = force
        mom_out[x] = moved[x] + 0.25 * force

    for copy in copies_q + copies_p:
        copy.wait_send()

    @pl.when(has_high)
    def _():
        up_w.wait_send()
        up_r.wait_send()

    @pl.when(has_low)
    def _():
        down_w.wait_send()
        down_r.wait_send()


def per_device(positions, momenta, forces, noise, masses, strengths, cell_counts, neighbour_cells):
    beads = lax.axis_size("bead")
    spaces = lax.axis_size("space")
    cells, slots = masses.shape
    wide = cells + 2 * HALO
    coef, kicks = propagator(beads)
    block = (3, cells, slots)
    f32 = jnp.float32
    vmem = pl.BlockSpec(memory_space=pltpu.VMEM)
    smem = pl.BlockSpec(memory_space=pltpu.SMEM)
    out = pl.pallas_call(
        functools.partial(kernel, beads, spaces, coef),
        out_shape=[jax.ShapeDtypeStruct(block, f32)] * 3,
        in_specs=[smem] * 3 + [vmem] * 6,
        out_specs=[vmem] * 3,
        scratch_shapes=[
            pltpu.VMEM((beads,) + block, f32),
            pltpu.VMEM((beads,) + block, f32),
            pltpu.VMEM((beads,) + block, f32),
            pltpu.VMEM((beads,) + block, f32),
            pltpu.VMEM(block, f32),
            pltpu.VMEM((cells, slots), f32),
            pltpu.VMEM((3, HALO, slots), f32),
            pltpu.VMEM((HALO, slots), f32),
            pltpu.VMEM((3, HALO, slots), f32),
            pltpu.VMEM((HALO, slots), f32),
            pltpu.VMEM((wide, 8, slots), f32),
            pltpu.VMEM((cells, 8, slots), f32),
            pltpu.VMEM((wide, 8, slots), f32),
            pltpu.VMEM((wide + 1, 48, slots), jnp.bfloat16),
            pltpu.VMEM((wide + 1, 16, slots), jnp.bfloat16),
            pltpu.VMEM((cells, 8, slots), f32),
            pltpu.SemaphoreType.DMA((beads,)),
            pltpu.SemaphoreType.DMA((beads,)),
            pltpu.SemaphoreType.DMA((beads,)),
            pltpu.SemaphoreType.DMA((beads,)),
            pltpu.SemaphoreType.DMA((4,)),
            pltpu.SemaphoreType.DMA((4,)),
        ],
        compiler_params=pltpu.CompilerParams(
            collective_id=0, has_side_effects=True, vmem_limit_bytes=32 * 1024 * 1024
        ),
    )(
        jnp.asarray(kicks),
        cell_counts,
        neighbour_cells,
        positions[0],
        momenta[0],
        forces[0],
        noise[0],
        masses,
        strengths,
    )
    return tuple(x[None] for x in out)


def solution(mesh):
    whole = P(("groups", "bead"), None, "space", None)
    in_specs = (
        whole,
        whole,
        whole,
        whole,
        P(("groups", "space"), None),
        P(("groups", "space"), None),
        P("groups"),
        P(("groups", "space"), None),
    )
    return jax.shard_map(
        per_device, mesh=mesh, in_specs=in_specs, out_specs=(whole,) * 3, check_vma=False
    )
```

time: 215 us -> 68.2 us (0.32)
  Pallas kernels: 0 us -> 59.2 us
  loops' own time: 49 us -> 0 us
  matrix products: 39 us -> 0 us
  other arithmetic: 38.6 us -> 0 us
  local copies, waits for them, and re-layouts: 31 us -> 7.72 us
  waiting for transfers between devices: 19.8 us -> 0 us
  between operations: 14.5 us -> 0.67 us
  blocking collectives: 11.4 us -> 0 us
  starting transfers between devices: 9.89 us -> 0 us
    pallas_call x0 -> x1, Pallas kernels: none -> 59.2 us  [per_device(): pl.pallas_call(functools.partial(kernel, beads, spaces, coef), out_shape=...]
    another operation x1 -> x0, loops' own time: 49 us -> none  [per_device(): result = lax.map(one_cell, (jnp.arange(ncells, dtype=jnp.int32), partners))]
    dot_general x25 -> x0, matrix products: 39 us -> none  [the longest x24 38.4 us: cell_force(): jnp.dot(kernel.reshape(slots, -1), far_coords.reshape(3, -1).T, precision...]
    reduce_sum x48 -> x0, other arithmetic: 27.5 us -> none  [the longest x24 16.2 us: cell_force(): jnp.sum((own_coords[:, :, None, None] - far_coords[:, None, :, :]) ** 2,...]
    reduce_scatter x1 -> x0, waiting for transfers between devices: 16.6 us -> none  [per_device(): lax.psum_scatter((coeff[:, None, None, None] * stacked[None]).reshape(6 *...]
    dynamic_slice x73 -> x0, local copies, waits for them, and re-layouts: 15.1 us -> none  [the longest x24 14.1 us: per_device(): result = lax.map(one_cell, (jnp.arange(ncells, dtype=jnp.int32), partners))]
    gather x24 -> x0, local copies, waits for them, and re-layouts: 14.5 us -> none  [one_cell(): gathered = widened[:, index_list]]
    all_gather x1 -> x0, blocking collectives: 11.4 us -> none  [per_device(): lax.all_gather(mode_pair, 'bead', axis=0, tiled=True)]
  transfers between devices with their start and end apart: 3 -> 0, of which waited for: 2 -> 0; matrix products, arithmetic and copies ran while one was open for 2% -> 0% of each run, Pallas kernels for 0% -> 0%
where the time goes in v1:
time: 68.2 us; the launch traced here: 67.6 us
  Pallas kernels  59.2 us (87%)
  local copies, waits for them, and re-layouts  7.72 us (11%)
    pallas_call x1, Pallas kernels, per_device(): pl.pallas_call(functools.partial(kernel, beads, spaces, coef), out_shape=...  59.2 us
    unnamed x21, local copies, waits for them, and re-layouts  7.72 us

profile of v1, /device:TPU:1, one launch (start us, length us, event | category | flops | bytes accessed | tf_op | source)
XLA Modules:
  0.0 67.6 jit_solution(3707238822024210329)
XLA Ops:
  0.6 0.0 copy-start.7
  0.6 0.0 copy-start.8
  0.7 0.7 copy-done.7
  1.3 0.0 copy-done.8
  1.3 0.0 copy-start
  1.3 0.8 %copy-done = f32[1,3,24,128]{3,2,1,0:T(8,128)S(1)} copy-done((f32[1,3,24,128]{3,2,1,0:T(8,128)S(1)}, f32[1,3,24,128]{3,2,1,0:T(8,128)}, u32[]{:S(2)}) %copy-start) | copy-done | bytes 36888
  2.1 0.0 copy-start.1
  2.1 0.8 %copy-done.1 = f32[1,3,24,128]{3,2,1,0:T(8,128)S(1)} copy-done((f32[1,3,24,128]{3,2,1,0:T(8,128)S(1)}, f32[1,3,24,128]{3,2,1,0:T(8,128)}, u32[]{:S(2)}) %copy-start.1) | copy-done | bytes 36888
  2.9 0.0 copy-start.2
  2.9 0.8 %copy-done.2 = f32[1,3,24,128]{3,2,1,0:T(8,128)S(1)} copy-done((f32[1,3,24,128]{3,2,1,0:T(8,128)S(1)}, f32[1,3,24,128]{3,2,1,0:T(8,128)}, u32[]{:S(2)}) %copy-start.2) | copy-done | bytes 36888
  3.6 0.0 copy-start.3
  3.6 0.8 %copy-done.3 = f32[1,3,24,128]{3,2,1,0:T(8,128)S(1)} copy-done((f32[1,3,24,128]{3,2,1,0:T(8,128)S(1)}, f32[1,3,24,128]{3,2,1,0:T(8,128)}, u32[]{:S(2)}) %copy-start.3) | copy-done | bytes 36888
  4.4 0.0 copy-start.4
  4.4 0.7 %copy-done.4 = s32[24,26]{1,0:T(8,128)S(1)} copy-done((s32[24,26]{1,0:T(8,128)S(1)}, s32[24,26]{1,0:T(8,128)}, u32[]{:S(2)}) %copy-start.4) | copy-done | bytes 2520
  5.1 0.0 copy-start.5
  5.1 0.7 %copy-done.5 = f32[24,128]{1,0:T(8,128)S(1)} copy-done((f32[24,128]{1,0:T(8,128)S(1)}, f32[24,128]{1,0:T(8,128)}, u32[]{:S(2)}) %copy-start.5) | copy-done | bytes 12312
  5.8 0.0 copy-start.6
  5.8 0.7 %copy-done.6 = f32[24,128]{1,0:T(8,128)S(1)} copy-done((f32[24,128]{1,0:T(8,128)S(1)}, f32[24,128]{1,0:T(8,128)}, u32[]{:S(2)}) %copy-start.6) | copy-done | bytes 12312
  6.5 59.2 %shard_map.112 = (f32[3,24,128]{2,1,0:T(8,128)S(1)}, f32[3,24,128]{2,1,0:T(8,128)S(1)}, f32[3,24,128]{2,1,0:T(8,128)S(1)}) custom-call(f32[2,4,4]{2,1,0:T(4,128)S(1)} %copy-done.7, s32[96]{0:T(128)S(1)} %copy-done.8, s32[24,26]{1,0:T(8,128)S(1)} %copy-done.4, f32[3,24,128]{2,1,0:T(8,128)S(1)} %bitcast.10, f32[3,24,128]{2,1,0:T(8,128)S(1)} %bitcast.11, ...), custom_call_target="tpu_custom_call" | custom-call | tf_op jit(solution)/shard_map/pallas_call | solution.py:344
  65.8 0.6 copy.15
  66.4 0.6 copy.16
  67.0 0.6 copy.17
Async XLA Ops:
  0.6 0.7 %copy-start.7 = (f32[2,4,4]{2,1,0:T(4,128)S(1)}, f32[2,4,4]{2,1,0:T(4,128)}, u32[]{:S(2)}) copy-start(f32[2,4,4]{2,1,0:T(4,128)} %constant.2.clone.kicks_ref) | copy-start | bytes 388
  0.6 0.7 %copy-start.8 = (s32[96]{0:T(128)S(1)}, s32[96]{0:T(128)}, u32[]{:S(2)}) copy-start(s32[96]{0:T(128)} %counts_ref.1) | copy-start | bytes 1156
  1.3 0.8 %copy-start = (f32[1,3,24,128]{3,2,1,0:T(8,128)S(1)}, f32[1,3,24,128]{3,2,1,0:T(8,128)}, u32[]{:S(2)}) copy-start(f32[1,3,24,128]{3,2,1,0:T(8,128)} %param.9) | copy-start | bytes 110596
  2.1 0.8 %copy-start.1 = (f32[1,3,24,128]{3,2,1,0:T(8,128)S(1)}, f32[1,3,24,128]{3,2,1,0:T(8,128)}, u32[]{:S(2)}) copy-start(f32[1,3,24,128]{3,2,1,0:T(8,128)} %param.10) | copy-start | bytes 110596
  2.9 0.8 %copy-start.2 = (f32[1,3,24,128]{3,2,1,0:T(8,128)S(1)}, f32[1,3,24,128]{3,2,1,0:T(8,128)}, u32[]{:S(2)}) copy-start(f32[1,3,24,128]{3,2,1,0:T(8,128)} %param.11) | copy-start | bytes 110596
  3.6 0.8 %copy-start.3 = (f32[1,3,24,128]{3,2,1,0:T(8,128)S(1)}, f32[1,3,24,128]{3,2,1,0:T(8,128)}, u32[]{:S(2)}) copy-start(f32[1,3,24,128]{3,2,1,0:T(8,128)} %param.12) | copy-start | bytes 110596
  4.4 0.7 %copy-start.4 = (s32[24,26]{1,0:T(8,128)S(1)}, s32[24,26]{1,0:T(8,128)}, u32[]{:S(2)}) copy-start(s32[24,26]{1,0:T(8,128)} %list_ref.1) | copy-start | bytes 7492
  5.1 0.7 %copy-start.5 = (f32[24,128]{1,0:T(8,128)S(1)}, f32[24,128]{1,0:T(8,128)}, u32[]{:S(2)}) copy-start(f32[24,128]{1,0:T(8,128)} %mass_ref.1) | copy-start | bytes 36868
  5.8 0.7 %copy-start.6 = (f32[24,128]{1,0:T(8,128)S(1)}, f32[24,128]{1,0:T(8,128)}, u32[]{:S(2)}) copy-start(f32[24,128]{1,0:T(8,128)} %str_ref.1) | copy-start | bytes 36868

commit v2 on v1

--- a/solution.py
+++ b/solution.py
@@ -239,15 +239,21 @@
         return scaled, norm
 
     def features(start, size):
-        for c in range(start, start + size, 8):
-            group = pl.ds(c, 8)
+        pad = jnp.zeros((slots - 48, slots), jnp.float32)
+
+        def group_of(g, carry):
+            group = pl.ds(pl.multiple_of(start + g * 8, 8), 8)
             high, mid, low = split3(rows_v[group])
-            far_b[group] = jnp.concatenate([high, high, mid, high, low, mid], axis=1).astype(
-                jnp.bfloat16
-            )
+            stacked = jnp.concatenate([high, high, mid, high, low, mid], axis=1)
             value = rows_w[group]
-            high = value.astype(jnp.bfloat16).astype(jnp.float32)
-            far_r[group] = jnp.concatenate([high, value - high], axis=1).astype(jnp.bfloat16)
+            near = value.astype(jnp.bfloat16).astype(jnp.float32)
+            far_r[group] = jnp.concatenate([near, value - near], axis=1).astype(jnp.bfloat16)
+            for i in range(8):
+                turned = jnp.transpose(jnp.concatenate([stacked[i], pad], axis=0))
+                far_b[start + g * 8 + i] = turned.astype(jnp.bfloat16)
+            return carry
+
+        lax.fori_loop(0, size // 8, group_of, 0)
 
     scaled, norm = place(HALO, cells, total, own_w[...])
     for x in range(3):
@@ -274,11 +280,7 @@
     def one_cell(c, carry):
         own = rows_u[c]
         high, mid, low = split3(own)
-        stacked = jnp.concatenate([high, mid, high, low, high, mid], axis=0)
-        stacked = jnp.concatenate(
-            [stacked, jnp.zeros((slots - stacked.shape[0], slots), jnp.float32)], axis=0
-        )
-        left = jnp.transpose(stacked)[:, :48].astype(jnp.bfloat16)
+        right = jnp.concatenate([high, mid, high, low, high, mid], axis=0).astype(jnp.bfloat16)
         partners = [c + HALO]
         for n in range(neigh):
             entry = list_ref[c, n]
@@ -286,20 +288,22 @@
             partners.append(jnp.where(entry >= 0, local, wide))
         if len(partners) % 2:
             partners.append(wide)
-        acc = jnp.zeros((16, slots), jnp.float32)
+        acc = jnp.zeros((16, 2 * slots), jnp.float32)
+        contract = (((1,), (0,)), ((), ()))
         for n in range(0, len(partners), 2):
             one, two = partners[n], partners[n + 1]
-            right = jnp.concatenate([far_b[one], far_b[two]], axis=1)
-            power = lax.dot_general(
-                left, right, (((1,), (0,)), ((), ())), preferred_element_type=jnp.float32
-            )
+            left = jnp.concatenate([far_b[one][:, :48], far_b[two][:, :48]], axis=0)
+            power = lax.dot_general(left, right, contract, preferred_element_type=jnp.float32)
             value = jnp.exp2(power)
             near = value.astype(jnp.bfloat16)
             rest = (value - near.astype(jnp.float32)).astype(jnp.bfloat16)
-            pulls = jnp.concatenate([far_r[one], far_r[two]], axis=1)
-            contract = (((1,), (1,)), ((), ()))
-            acc = acc + lax.dot_general(pulls, near, contract, preferred_element_type=jnp.float32)
-            acc = acc + lax.dot_general(pulls, rest, contract, preferred_element_type=jnp.float32)
+            acc = acc + lax.dot_general(
+                jnp.concatenate([far_r[one], far_r[two]], axis=1),
+                jnp.concatenate([near, rest], axis=1),
+                contract,
+                preferred_element_type=jnp.float32,
+            )
+        acc = acc[:, :slots] + acc[:, slots:]
         sums = acc[0:8] + acc[8:16]
         weight = rows_w[c + HALO][3:4]
         rows_f[c] = (PAIR_SCALE / ROOT) * weight * (own * sums[3:4] - sums)
@@ -360,7 +364,7 @@
             pltpu.VMEM((wide, 8, slots), f32),
             pltpu.VMEM((cells, 8, slots), f32),
             pltpu.VMEM((wide, 8, slots), f32),
-            pltpu.VMEM((wide + 1, 48, slots), jnp.bfloat16),
+            pltpu.VMEM((wide + 1, slots, slots), jnp.bfloat16),
             pltpu.VMEM((wide + 1, 16, slots), jnp.bfloat16),
             pltpu.VMEM((cells, 8, slots), f32),
             pltpu.SemaphoreType.DMA((beads,)),

time: 68.2 us -> 40.7 us (0.60)
  Pallas kernels: 59.2 us -> 31.8 us
    pallas_call x1, Pallas kernels: 59.2 us -> 31.8 us  [per_device(): pl.pallas_call(functools.partial(kernel, beads, spaces, coef), out_shape=...]
where the time goes in v2:
time: 40.7 us; the launch traced here: 40.2 us
  Pallas kernels  31.8 us (78%)
  local copies, waits for them, and re-layouts  7.72 us (19%)
  between operations  0.67 us (2%)
    pallas_call x1, Pallas kernels, per_device(): pl.pallas_call(functools.partial(kernel, beads, spaces, coef), out_shape=...  31.8 us
    unnamed x21, local copies, waits for them, and re-layouts  7.72 us

profile of v2, /device:TPU:1, one launch (start us, length us, event | category | flops | bytes accessed | tf_op | source)
XLA Modules:
  0.0 40.2 jit_solution(13423119029975388432)
XLA Ops:
  0.6 0.0 copy-start.7
  0.6 0.0 copy-start.8
  0.7 0.7 %copy-done.7 = f32[2,4,4]{2,1,0:T(4,128)S(1)} copy-done((f32[2,4,4]{2,1,0:T(4,128)S(1)}, f32[2,4,4]{2,1,0:T(4,128)}, u32[]{:S(2)}) %copy-start.7) | copy-done | bytes 152
  1.3 0.0 copy-done.8
  1.3 0.0 copy-start
  1.3 0.8 %copy-done = f32[1,3,24,128]{3,2,1,0:T(8,128)S(1)} copy-done((f32[1,3,24,128]{3,2,1,0:T(8,128)S(1)}, f32[1,3,24,128]{3,2,1,0:T(8,128)}, u32[]{:S(2)}) %copy-start) | copy-done | bytes 36888
  2.1 0.0 copy-start.1
  2.1 0.8 %copy-done.1 = f32[1,3,24,128]{3,2,1,0:T(8,128)S(1)} copy-done((f32[1,3,24,128]{3,2,1,0:T(8,128)S(1)}, f32[1,3,24,128]{3,2,1,0:T(8,128)}, u32[]{:S(2)}) %copy-start.1) | copy-done | bytes 36888
  2.9 0.0 copy-start.2
  2.9 0.8 %copy-done.2 = f32[1,3,24,128]{3,2,1,0:T(8,128)S(1)} copy-done((f32[1,3,24,128]{3,2,1,0:T(8,128)S(1)}, f32[1,3,24,128]{3,2,1,0:T(8,128)}, u32[]{:S(2)}) %copy-start.2) | copy-done | bytes 36888
  3.6 0.0 copy-start.3
  3.6 0.8 %copy-done.3 = f32[1,3,24,128]{3,2,1,0:T(8,128)S(1)} copy-done((f32[1,3,24,128]{3,2,1,0:T(8,128)S(1)}, f32[1,3,24,128]{3,2,1,0:T(8,128)}, u32[]{:S(2)}) %copy-start.3) | copy-done | bytes 36888
  4.4 0.0 copy-start.4
  4.4 0.7 %copy-done.4 = s32[24,26]{1,0:T(8,128)S(1)} copy-done((s32[24,26]{1,0:T(8,128)S(1)}, s32[24,26]{1,0:T(8,128)}, u32[]{:S(2)}) %copy-start.4) | copy-done | bytes 2520
  5.1 0.0 copy-start.5
  5.1 0.7 %copy-done.5 = f32[24,128]{1,0:T(8,128)S(1)} copy-done((f32[24,128]{1,0:T(8,128)S(1)}, f32[24,128]{1,0:T(8,128)}, u32[]{:S(2)}) %copy-start.5) | copy-done | bytes 12312
  5.8 0.0 copy-start.6
  5.8 0.7 %copy-done.6 = f32[24,128]{1,0:T(8,128)S(1)} copy-done((f32[24,128]{1,0:T(8,128)S(1)}, f32[24,128]{1,0:T(8,128)}, u32[]{:S(2)}) %copy-start.6) | copy-done | bytes 12312
  6.5 31.8 %shard_map.112 = (f32[3,24,128]{2,1,0:T(8,128)S(1)}, f32[3,24,128]{2,1,0:T(8,128)S(1)}, f32[3,24,128]{2,1,0:T(8,128)S(1)}) custom-call(f32[2,4,4]{2,1,0:T(4,128)S(1)} %copy-done.7, s32[96]{0:T(128)S(1)} %copy-done.8, s32[24,26]{1,0:T(8,128)S(1)} %copy-done.4, f32[3,24,128]{2,1,0:T(8,128)S(1)} %bitcast.10, f32[3,24,128]{2,1,0:T(8,128)S(1)} %bitcast.11, ...), custom_call_target="tpu_custom_call" | custom-call | tf_op jit(solution)/shard_map/pallas_call | solution.py:348
  38.3 0.6 %copy.15 = f32[1,3,24,128]{3,2,1,0:T(8,128)} copy(f32[1,3,24,128]{3,2,1,0:T(8,128)S(1)} %bitcast.9) | data formatting | bytes 73728
  39.0 0.6 %copy.16 = f32[1,3,24,128]{3,2,1,0:T(8,128)} copy(f32[1,3,24,128]{3,2,1,0:T(8,128)S(1)} %bitcast.8) | data formatting | bytes 73728
  39.6 0.6 %copy.17 = f32[1,3,24,128]{3,2,1,0:T(8,128)} copy(f32[1,3,24,128]{3,2,1,0:T(8,128)S(1)} %bitcast.7) | data formatting | bytes 73728
Async XLA Ops:
  0.6 0.7 %copy-start.7 = (f32[2,4,4]{2,1,0:T(4,128)S(1)}, f32[2,4,4]{2,1,0:T(4,128)}, u32[]{:S(2)}) copy-start(f32[2,4,4]{2,1,0:T(4,128)} %constant.2.clone.kicks_ref) | copy-start | bytes 388
  0.6 0.7 %copy-start.8 = (s32[96]{0:T(128)S(1)}, s32[96]{0:T(128)}, u32[]{:S(2)}) copy-start(s32[96]{0:T(128)} %counts_ref.1) | copy-start | bytes 1156
  1.3 0.8 %copy-start = (f32[1,3,24,128]{3,2,1,0:T(8,128)S(1)}, f32[1,3,24,128]{3,2,1,0:T(8,128)}, u32[]{:S(2)}) copy-start(f32[1,3,24,128]{3,2,1,0:T(8,128)} %param.9) | copy-start | bytes 110596
  2.1 0.8 %copy-start.1 = (f32[1,3,24,128]{3,2,1,0:T(8,128)S(1)}, f32[1,3,24,128]{3,2,1,0:T(8,128)}, u32[]{:S(2)}) copy-start(f32[1,3,24,128]{3,2,1,0:T(8,128)} %param.10) | copy-start | bytes 110596
  2.9 0.8 %copy-start.2 = (f32[1,3,24,128]{3,2,1,0:T(8,128)S(1)}, f32[1,3,24,128]{3,2,1,0:T(8,128)}, u32[]{:S(2)}) copy-start(f32[1,3,24,128]{3,2,1,0:T(8,128)} %param.11) | copy-start | bytes 110596
  3.6 0.8 %copy-start.3 = (f32[1,3,24,128]{3,2,1,0:T(8,128)S(1)}, f32[1,3,24,128]{3,2,1,0:T(8,128)}, u32[]{:S(2)}) copy-start(f32[1,3,24,128]{3,2,1,0:T(8,128)} %param.12) | copy-start | bytes 110596
  4.4 0.7 %copy-start.4 = (s32[24,26]{1,0:T(8,128)S(1)}, s32[24,26]{1,0:T(8,128)}, u32[]{:S(2)}) copy-start(s32[24,26]{1,0:T(8,128)} %list_ref.1) | copy-start | bytes 7492
  5.1 0.7 %copy-start.5 = (f32[24,128]{1,0:T(8,128)S(1)}, f32[24,128]{1,0:T(8,128)}, u32[]{:S(2)}) copy-start(f32[24,128]{1,0:T(8,128)} %mass_ref.1) | copy-start | bytes 36868
  5.8 0.7 %copy-start.6 = (f32[24,128]{1,0:T(8,128)S(1)}, f32[24,128]{1,0:T(8,128)}, u32[]{:S(2)}) copy-start(f32[24,128]{1,0:T(8,128)} %str_ref.1) | copy-start | bytes 36868

commit v3 on v2

--- a/solution.py
+++ b/solution.py
@@ -99,6 +99,7 @@
     far_b,
     far_r,
     rows_f,
+    listed,
     sq_sem,
     rq_sem,
     sp_sem,
@@ -207,8 +208,14 @@
     rows_v[...] = jnp.zeros_like(rows_v)
     rows_u[...] = jnp.zeros_like(rows_u)
     rows_w[...] = jnp.zeros_like(rows_w)
-    far_b[wide] = jnp.zeros(far_b.shape[1:], far_b.dtype)
-    far_r[wide] = jnp.zeros(far_r.shape[1:], far_r.dtype)
+    entries = list_ref[...]
+    row = lax.broadcasted_iota(jnp.int32, (cells, 1), 0) + space * cells
+    shifted = jnp.where(entries >= 0, entries - row + HALO + 1, -1)
+    column = lax.broadcasted_iota(jnp.int32, (cells, slots), 1)
+    found = column == HALO + 1
+    for n in range(neigh):
+        found = jnp.logical_or(found, shifted[:, n : n + 1] == column)
+    listed[...] = jnp.where(found, 1.0, 0.0)
 
     for copy in copies_q:
         copy.wait_recv()
@@ -277,39 +284,48 @@
     place(HALO + cells, HALO, high_r[...], high_w[...])
     features(HALO + cells, HALO)
 
-    def one_cell(c, carry):
-        own = rows_u[c]
-        high, mid, low = split3(own)
-        right = jnp.concatenate([high, mid, high, low, high, mid], axis=0).astype(jnp.bfloat16)
-        partners = [c + HALO]
-        for n in range(neigh):
-            entry = list_ref[c, n]
-            local = jnp.clip(entry - space * cells + HALO, 0, wide - 1)
-            partners.append(jnp.where(entry >= 0, local, wide))
-        if len(partners) % 2:
-            partners.append(wide)
-        acc = jnp.zeros((16, 2 * slots), jnp.float32)
-        contract = (((1,), (0,)), ((), ()))
-        for n in range(0, len(partners), 2):
-            one, two = partners[n], partners[n + 1]
-            left = jnp.concatenate([far_b[one][:, :48], far_b[two][:, :48]], axis=0)
+    def own_part(c):
+        high, mid, low = split3(rows_u[c])
+        return jnp.concatenate([high, mid, high, low, high, mid], axis=0).astype(jnp.bfloat16)
+
+    contract = (((1,), (0,)), ((), ()))
+
+    def one_pair(pair, carry):
+        c = 2 * pair
+        right = jnp.concatenate([own_part(c), own_part(c + 1)], axis=1)
+        flags = listed[pl.ds(c, 1), :], listed[pl.ds(c + 1, 1), :]
+
+        def pulls(t, which):
+            flag = flags[which][:, t + 1 - which : t + 2 - which]
+            return far_r[c + t] * jnp.broadcast_to(flag, (16, slots)).astype(jnp.bfloat16)
+
+        acc = jnp.zeros((32, 4 * slots), jnp.float32)
+        for t in range(0, 2 * HALO + 2, 2):
+            left = jnp.concatenate([far_b[c + t][:, :48], far_b[c + t + 1][:, :48]], axis=0)
             power = lax.dot_general(left, right, contract, preferred_element_type=jnp.float32)
             value = jnp.exp2(power)
             near = value.astype(jnp.bfloat16)
             rest = (value - near.astype(jnp.float32)).astype(jnp.bfloat16)
+            sides = [
+                jnp.concatenate([pulls(t + i, which) for which in range(2)], axis=0)
+                for i in range(2)
+            ]
             acc = acc + lax.dot_general(
-                jnp.concatenate([far_r[one], far_r[two]], axis=1),
+                jnp.concatenate(sides, axis=1),
                 jnp.concatenate([near, rest], axis=1),
                 contract,
                 preferred_element_type=jnp.float32,
             )
-        acc = acc[:, :slots] + acc[:, slots:]
-        sums = acc[0:8] + acc[8:16]
-        weight = rows_w[c + HALO][3:4]
-        rows_f[c] = (PAIR_SCALE / ROOT) * weight * (own * sums[3:4] - sums)
+        acc = acc[:, : 2 * slots] + acc[:, 2 * slots :]
+        for which in range(2):
+            part = acc[16 * which : 16 * which + 16, which * slots : (which + 1) * slots]
+            sums = part[0:8] + part[8:16]
+            own = rows_u[c + which]
+            weight = rows_w[c + which + HALO][3:4]
+            rows_f[c + which] = (PAIR_SCALE / ROOT) * weight * (own * sums[3:4] - sums)
         return carry
 
-    lax.fori_loop(0, cells, one_cell, 0)
+    lax.fori_loop(0, cells // 2, one_pair, 0)
 
     for copy in copies_p:
         copy.wait_recv()
@@ -348,7 +364,7 @@
     out = pl.pallas_call(
         functools.partial(kernel, beads, spaces, coef),
         out_shape=[jax.ShapeDtypeStruct(block, f32)] * 3,
-        in_specs=[smem] * 3 + [vmem] * 6,
+        in_specs=[smem] * 2 + [vmem] * 7,
         out_specs=[vmem] * 3,
         scratch_shapes=[
             pltpu.VMEM((beads,) + block, f32),
@@ -364,9 +380,10 @@
             pltpu.VMEM((wide, 8, slots), f32),
             pltpu.VMEM((cells, 8, slots), f32),
             pltpu.VMEM((wide, 8, slots), f32),
-            pltpu.VMEM((wide + 1, slots, slots), jnp.bfloat16),
-            pltpu.VMEM((wide + 1, 16, slots), jnp.bfloat16),
+            pltpu.VMEM((wide, slots, slots), jnp.bfloat16),
+            pltpu.VMEM((wide, 16, slots), jnp.bfloat16),
             pltpu.VMEM((cells, 8, slots), f32),
+            pltpu.VMEM((cells, slots), f32),
             pltpu.SemaphoreType.DMA((beads,)),
             pltpu.SemaphoreType.DMA((beads,)),
             pltpu.SemaphoreType.DMA((beads,)),

time: 40.7 us -> 43.2 us (1.061)
  Pallas kernels: 31.8 us -> 34.3 us
    pallas_call x1, Pallas kernels: 31.8 us -> 34.3 us  [per_device(): pl.pallas_call(functools.partial(kernel, beads, spaces, coef), out_shape=...]
where the time goes in v3:
time: 43.2 us; the launch traced here: 42.7 us
  Pallas kernels  34.3 us (79%)
  local copies, waits for them, and re-layouts  7.72 us (18%)
  between operations  0.67 us (2%)
    pallas_call x1, Pallas kernels, per_device(): pl.pallas_call(functools.partial(kernel, beads, spaces, coef), out_shape=...  34.3 us
    unnamed x21, local copies, waits for them, and re-layouts  7.72 us

profile of v3, /device:TPU:1, one launch (start us, length us, event | category | flops | bytes accessed | tf_op | source)
XLA Modules:
  0.0 42.7 jit_solution(6240464646742854083)
XLA Ops:
  0.6 0.0 copy-start.7
  0.6 0.0 copy-start.8
  0.7 0.7 %copy-done.7 = f32[2,4,4]{2,1,0:T(4,128)S(1)} copy-done((f32[2,4,4]{2,1,0:T(4,128)S(1)}, f32[2,4,4]{2,1,0:T(4,128)}, u32[]{:S(2)}) %copy-start.7) | copy-done | bytes 152
  1.3 0.0 copy-done.8
  1.3 0.0 copy-start
  1.3 0.8 %copy-done = f32[1,3,24,128]{3,2,1,0:T(8,128)S(1)} copy-done((f32[1,3,24,128]{3,2,1,0:T(8,128)S(1)}, f32[1,3,24,128]{3,2,1,0:T(8,128)}, u32[]{:S(2)}) %copy-start) | copy-done | bytes 36888
  2.1 0.0 copy-start.1
  2.1 0.8 %copy-done.1 = f32[1,3,24,128]{3,2,1,0:T(8,128)S(1)} copy-done((f32[1,3,24,128]{3,2,1,0:T(8,128)S(1)}, f32[1,3,24,128]{3,2,1,0:T(8,128)}, u32[]{:S(2)}) %copy-start.1) | copy-done | bytes 36888
  2.9 0.0 copy-start.2
  2.9 0.8 %copy-done.2 = f32[1,3,24,128]{3,2,1,0:T(8,128)S(1)} copy-done((f32[1,3,24,128]{3,2,1,0:T(8,128)S(1)}, f32[1,3,24,128]{3,2,1,0:T(8,128)}, u32[]{:S(2)}) %copy-start.2) | copy-done | bytes 36888
  3.6 0.0 copy-start.3
  3.6 0.8 %copy-done.3 = f32[1,3,24,128]{3,2,1,0:T(8,128)S(1)} copy-done((f32[1,3,24,128]{3,2,1,0:T(8,128)S(1)}, f32[1,3,24,128]{3,2,1,0:T(8,128)}, u32[]{:S(2)}) %copy-start.3) | copy-done | bytes 36888
  4.4 0.0 copy-start.4
  4.4 0.7 %copy-done.4 = s32[24,26]{1,0:T(8,128)S(1)} copy-done((s32[24,26]{1,0:T(8,128)S(1)}, s32[24,26]{1,0:T(8,128)}, u32[]{:S(2)}) %copy-start.4) | copy-done | bytes 2520
  5.1 0.0 copy-start.5
  5.1 0.7 %copy-done.5 = f32[24,128]{1,0:T(8,128)S(1)} copy-done((f32[24,128]{1,0:T(8,128)S(1)}, f32[24,128]{1,0:T(8,128)}, u32[]{:S(2)}) %copy-start.5) | copy-done | bytes 12312
  5.8 0.0 copy-start.6
  5.8 0.7 %copy-done.6 = f32[24,128]{1,0:T(8,128)S(1)} copy-done((f32[24,128]{1,0:T(8,128)S(1)}, f32[24,128]{1,0:T(8,128)}, u32[]{:S(2)}) %copy-start.6) | copy-done | bytes 12312
  6.5 34.3 %shard_map.112 = (f32[3,24,128]{2,1,0:T(8,128)S(1)}, f32[3,24,128]{2,1,0:T(8,128)S(1)}, f32[3,24,128]{2,1,0:T(8,128)S(1)}) custom-call(f32[2,4,4]{2,1,0:T(4,128)S(1)} %copy-done.7, s32[96]{0:T(128)S(1)} %copy-done.8, s32[24,26]{1,0:T(8,128)S(1)} %copy-done.4, f32[3,24,128]{2,1,0:T(8,128)S(1)} %bitcast.10, f32[3,24,128]{2,1,0:T(8,128)S(1)} %bitcast.11, ...), custom_call_target="tpu_custom_call" | custom-call | tf_op jit(solution)/shard_map/pallas_call | solution.py:364
  40.8 0.6 %copy.15 = f32[1,3,24,128]{3,2,1,0:T(8,128)} copy(f32[1,3,24,128]{3,2,1,0:T(8,128)S(1)} %bitcast.9) | data formatting | bytes 73728
  41.4 0.6 %copy.16 = f32[1,3,24,128]{3,2,1,0:T(8,128)} copy(f32[1,3,24,128]{3,2,1,0:T(8,128)S(1)} %bitcast.8) | data formatting | bytes 73728
  42.1 0.6 %copy.17 = f32[1,3,24,128]{3,2,1,0:T(8,128)} copy(f32[1,3,24,128]{3,2,1,0:T(8,128)S(1)} %bitcast.7) | data formatting | bytes 73728
Async XLA Ops:
  0.6 0.7 %copy-start.7 = (f32[2,4,4]{2,1,0:T(4,128)S(1)}, f32[2,4,4]{2,1,0:T(4,128)}, u32[]{:S(2)}) copy-start(f32[2,4,4]{2,1,0:T(4,128)} %constant.2.clone.kicks_ref) | copy-start | bytes 388
  0.6 0.7 %copy-start.8 = (s32[96]{0:T(128)S(1)}, s32[96]{0:T(128)}, u32[]{:S(2)}) copy-start(s32[96]{0:T(128)} %counts_ref.1) | copy-start | bytes 1156
  1.3 0.8 %copy-start = (f32[1,3,24,128]{3,2,1,0:T(8,128)S(1)}, f32[1,3,24,128]{3,2,1,0:T(8,128)}, u32[]{:S(2)}) copy-start(f32[1,3,24,128]{3,2,1,0:T(8,128)} %param.9) | copy-start | bytes 110596
  2.1 0.8 %copy-start.1 = (f32[1,3,24,128]{3,2,1,0:T(8,128)S(1)}, f32[1,3,24,128]{3,2,1,0:T(8,128)}, u32[]{:S(2)}) copy-start(f32[1,3,24,128]{3,2,1,0:T(8,128)} %param.10) | copy-start | bytes 110596
  2.9 0.8 %copy-start.2 = (f32[1,3,24,128]{3,2,1,0:T(8,128)S(1)}, f32[1,3,24,128]{3,2,1,0:T(8,128)}, u32[]{:S(2)}) copy-start(f32[1,3,24,128]{3,2,1,0:T(8,128)} %param.11) | copy-start | bytes 110596
  3.6 0.8 %copy-start.3 = (f32[1,3,24,128]{3,2,1,0:T(8,128)S(1)}, f32[1,3,24,128]{3,2,1,0:T(8,128)}, u32[]{:S(2)}) copy-start(f32[1,3,24,128]{3,2,1,0:T(8,128)} %param.12) | copy-start | bytes 110596
  4.4 0.7 %copy-start.4 = (s32[24,26]{1,0:T(8,128)S(1)}, s32[24,26]{1,0:T(8,128)}, u32[]{:S(2)}) copy-start(s32[24,26]{1,0:T(8,128)} %list_ref.1) | copy-start | bytes 7492
  5.1 0.7 %copy-start.5 = (f32[24,128]{1,0:T(8,128)S(1)}, f32[24,128]{1,0:T(8,128)}, u32[]{:S(2)}) copy-start(f32[24,128]{1,0:T(8,128)} %mass_ref.1) | copy-start | bytes 36868
  5.8 0.7 %copy-start.6 = (f32[24,128]{1,0:T(8,128)S(1)}, f32[24,128]{1,0:T(8,128)}, u32[]{:S(2)}) copy-start(f32[24,128]{1,0:T(8,128)} %str_ref.1) | copy-start | bytes 36868

commit v4 on v2

--- a/solution.py
+++ b/solution.py
@@ -253,7 +253,7 @@
                 far_b[start + g * 8 + i] = turned.astype(jnp.bfloat16)
             return carry
 
-        lax.fori_loop(0, size // 8, group_of, 0)
+        lax.fori_loop(0, size // 8, group_of, 0, unroll=True)
 
     scaled, norm = place(HALO, cells, total, own_w[...])
     for x in range(3):
@@ -309,7 +309,7 @@
         rows_f[c] = (PAIR_SCALE / ROOT) * weight * (own * sums[3:4] - sums)
         return carry
 
-    lax.fori_loop(0, cells, one_cell, 0)
+    lax.fori_loop(0, cells, one_cell, 0, unroll=4)
 
     for copy in copies_p:
         copy.wait_recv()

time: 40.7 us -> 36.1 us (0.89)
  Pallas kernels: 31.8 us -> 27.2 us
    pallas_call x1, Pallas kernels: 31.8 us -> 27.2 us  [per_device(): pl.pallas_call(functools.partial(kernel, beads, spaces, coef), out_shape=...]
where the time goes in v4:
time: 36.1 us; the launch traced here: 35.6 us
  Pallas kernels  27.2 us (75%)
  local copies, waits for them, and re-layouts  7.72 us (21%)
  between operations  0.67 us (2%)
    pallas_call x1, Pallas kernels, per_device(): pl.pallas_call(functools.partial(kernel, beads, spaces, coef), out_shape=...  27.2 us
    unnamed x21, local copies, waits for them, and re-layouts  7.72 us

profile of v4, /device:TPU:1, one launch (start us, length us, event | category | flops | bytes accessed | tf_op | source)
XLA Modules:
  0.0 35.6 jit_solution(17992789664444061352)
XLA Ops:
  0.6 0.0 copy-start.7
  0.6 0.0 copy-start.8
  0.7 0.7 %copy-done.7 = f32[2,4,4]{2,1,0:T(4,128)S(1)} copy-done((f32[2,4,4]{2,1,0:T(4,128)S(1)}, f32[2,4,4]{2,1,0:T(4,128)}, u32[]{:S(2)}) %copy-start.7) | copy-done | bytes 152
  1.3 0.0 copy-done.8
  1.3 0.0 copy-start
  1.3 0.8 %copy-done = f32[1,3,24,128]{3,2,1,0:T(8,128)S(1)} copy-done((f32[1,3,24,128]{3,2,1,0:T(8,128)S(1)}, f32[1,3,24,128]{3,2,1,0:T(8,128)}, u32[]{:S(2)}) %copy-start) | copy-done | bytes 36888
  2.1 0.0 copy-start.1
  2.1 0.8 %copy-done.1 = f32[1,3,24,128]{3,2,1,0:T(8,128)S(1)} copy-done((f32[1,3,24,128]{3,2,1,0:T(8,128)S(1)}, f32[1,3,24,128]{3,2,1,0:T(8,128)}, u32[]{:S(2)}) %copy-start.1) | copy-done | bytes 36888
  2.9 0.0 copy-start.2
  2.9 0.8 %copy-done.2 = f32[1,3,24,128]{3,2,1,0:T(8,128)S(1)} copy-done((f32[1,3,24,128]{3,2,1,0:T(8,128)S(1)}, f32[1,3,24,128]{3,2,1,0:T(8,128)}, u32[]{:S(2)}) %copy-start.2) | copy-done | bytes 36888
  3.6 0.0 copy-start.3
  3.6 0.8 %copy-done.3 = f32[1,3,24,128]{3,2,1,0:T(8,128)S(1)} copy-done((f32[1,3,24,128]{3,2,1,0:T(8,128)S(1)}, f32[1,3,24,128]{3,2,1,0:T(8,128)}, u32[]{:S(2)}) %copy-start.3) | copy-done | bytes 36888
  4.4 0.0 copy-start.4
  4.4 0.7 %copy-done.4 = s32[24,26]{1,0:T(8,128)S(1)} copy-done((s32[24,26]{1,0:T(8,128)S(1)}, s32[24,26]{1,0:T(8,128)}, u32[]{:S(2)}) %copy-start.4) | copy-done | bytes 2520
  5.1 0.0 copy-start.5
  5.1 0.7 %copy-done.5 = f32[24,128]{1,0:T(8,128)S(1)} copy-done((f32[24,128]{1,0:T(8,128)S(1)}, f32[24,128]{1,0:T(8,128)}, u32[]{:S(2)}) %copy-start.5) | copy-done | bytes 12312
  5.8 0.0 copy-start.6
  5.8 0.7 %copy-done.6 = f32[24,128]{1,0:T(8,128)S(1)} copy-done((f32[24,128]{1,0:T(8,128)S(1)}, f32[24,128]{1,0:T(8,128)}, u32[]{:S(2)}) %copy-start.6) | copy-done | bytes 12312
  6.5 27.2 %shard_map.112 = (f32[3,24,128]{2,1,0:T(8,128)S(1)}, f32[3,24,128]{2,1,0:T(8,128)S(1)}, f32[3,24,128]{2,1,0:T(8,128)S(1)}) custom-call(f32[2,4,4]{2,1,0:T(4,128)S(1)} %copy-done.7, s32[96]{0:T(128)S(1)} %copy-done.8, s32[24,26]{1,0:T(8,128)S(1)} %copy-done.4, f32[3,24,128]{2,1,0:T(8,128)S(1)} %bitcast.10, f32[3,24,128]{2,1,0:T(8,128)S(1)} %bitcast.11, ...), custom_call_target="tpu_custom_call" | custom-call | tf_op jit(solution)/shard_map/pallas_call | solution.py:348
  33.7 0.6 %copy.15 = f32[1,3,24,128]{3,2,1,0:T(8,128)} copy(f32[1,3,24,128]{3,2,1,0:T(8,128)S(1)} %bitcast.9) | data formatting | bytes 73728
  34.3 0.6 %copy.16 = f32[1,3,24,128]{3,2,1,0:T(8,128)} copy(f32[1,3,24,128]{3,2,1,0:T(8,128)S(1)} %bitcast.8) | data formatting | bytes 73728
  34.9 0.6 %copy.17 = f32[1,3,24,128]{3,2,1,0:T(8,128)} copy(f32[1,3,24,128]{3,2,1,0:T(8,128)S(1)} %bitcast.7) | data formatting | bytes 73728
Async XLA Ops:
  0.6 0.7 %copy-start.7 = (f32[2,4,4]{2,1,0:T(4,128)S(1)}, f32[2,4,4]{2,1,0:T(4,128)}, u32[]{:S(2)}) copy-start(f32[2,4,4]{2,1,0:T(4,128)} %constant.2.clone.kicks_ref) | copy-start | bytes 388
  0.6 0.7 %copy-start.8 = (s32[96]{0:T(128)S(1)}, s32[96]{0:T(128)}, u32[]{:S(2)}) copy-start(s32[96]{0:T(128)} %counts_ref.1) | copy-start | bytes 1156
  1.3 0.8 %copy-start = (f32[1,3,24,128]{3,2,1,0:T(8,128)S(1)}, f32[1,3,24,128]{3,2,1,0:T(8,128)}, u32[]{:S(2)}) copy-start(f32[1,3,24,128]{3,2,1,0:T(8,128)} %param.9) | copy-start | bytes 110596
  2.1 0.8 %copy-start.1 = (f32[1,3,24,128]{3,2,1,0:T(8,128)S(1)}, f32[1,3,24,128]{3,2,1,0:T(8,128)}, u32[]{:S(2)}) copy-start(f32[1,3,24,128]{3,2,1,0:T(8,128)} %param.10) | copy-start | bytes 110596
  2.9 0.8 %copy-start.2 = (f32[1,3,24,128]{3,2,1,0:T(8,128)S(1)}, f32[1,3,24,128]{3,2,1,0:T(8,128)}, u32[]{:S(2)}) copy-start(f32[1,3,24,128]{3,2,1,0:T(8,128)} %param.11) | copy-start | bytes 110596
  3.6 0.8 %copy-start.3 = (f32[1,3,24,128]{3,2,1,0:T(8,128)S(1)}, f32[1,3,24,128]{3,2,1,0:T(8,128)}, u32[]{:S(2)}) copy-start(f32[1,3,24,128]{3,2,1,0:T(8,128)} %param.12) | copy-start | bytes 110596
  4.4 0.7 %copy-start.4 = (s32[24,26]{1,0:T(8,128)S(1)}, s32[24,26]{1,0:T(8,128)}, u32[]{:S(2)}) copy-start(s32[24,26]{1,0:T(8,128)} %list_ref.1) | copy-start | bytes 7492
  5.1 0.7 %copy-start.5 = (f32[24,128]{1,0:T(8,128)S(1)}, f32[24,128]{1,0:T(8,128)}, u32[]{:S(2)}) copy-start(f32[24,128]{1,0:T(8,128)} %mass_ref.1) | copy-start | bytes 36868
  5.8 0.7 %copy-start.6 = (f32[24,128]{1,0:T(8,128)S(1)}, f32[24,128]{1,0:T(8,128)}, u32[]{:S(2)}) copy-start(f32[24,128]{1,0:T(8,128)} %str_ref.1) | copy-start | bytes 36868

commit v5 on v4

--- a/solution.py
+++ b/solution.py
@@ -191,8 +191,6 @@
     for d in range(beads):
         target = lax.rem(bead + d, beads)
         send_p[d] = coef["pq"][d] * mass_q + coef["pp"][d] * p + kicks_ref[1, bead, target] * noise_p
-    for copy in copies_p:
-        copy.start()
 
     @pl.when(jnp.logical_not(has_low))
     def _():
@@ -225,6 +223,9 @@
     @pl.when(has_low)
     def _():
         down_r.start()
+
+    for copy in copies_p:
+        copy.start()
 
     def place(start, size, coords, weights):
         scaled = ROOT * coords

time: 36.1 us -> 35.2 us (0.975)
  Pallas kernels: 27.2 us -> 26.2 us
    pallas_call x1, Pallas kernels: 27.2 us -> 26.2 us  [per_device(): pl.pallas_call(functools.partial(kernel, beads, spaces, coef), out_shape=...]
where the time goes in v5:
time: 35.2 us; the launch traced here: 34.6 us
  Pallas kernels  26.2 us (74%)
  local copies, waits for them, and re-layouts  7.72 us (22%)
  between operations  0.67 us (2%)
    pallas_call x1, Pallas kernels, per_device(): pl.pallas_call(functools.partial(kernel, beads, spaces, coef), out_shape=...  26.2 us
    unnamed x21, local copies, waits for them, and re-layouts  7.72 us

profile of v5, /device:TPU:1, one launch (start us, length us, event | category | flops | bytes accessed | tf_op | source)
XLA Modules:
  0.0 34.6 jit_solution(7733512080008917812)
XLA Ops:
  0.6 0.0 copy-start.7
  0.6 0.0 copy-start.8
  0.7 0.7 %copy-done.7 = f32[2,4,4]{2,1,0:T(4,128)S(1)} copy-done((f32[2,4,4]{2,1,0:T(4,128)S(1)}, f32[2,4,4]{2,1,0:T(4,128)}, u32[]{:S(2)}) %copy-start.7) | copy-done | bytes 152
  1.3 0.0 copy-done.8
  1.3 0.0 copy-start
  1.3 0.8 %copy-done = f32[1,3,24,128]{3,2,1,0:T(8,128)S(1)} copy-done((f32[1,3,24,128]{3,2,1,0:T(8,128)S(1)}, f32[1,3,24,128]{3,2,1,0:T(8,128)}, u32[]{:S(2)}) %copy-start) | copy-done | bytes 36888
  2.1 0.0 copy-start.1
  2.1 0.8 %copy-done.1 = f32[1,3,24,128]{3,2,1,0:T(8,128)S(1)} copy-done((f32[1,3,24,128]{3,2,1,0:T(8,128)S(1)}, f32[1,3,24,128]{3,2,1,0:T(8,128)}, u32[]{:S(2)}) %copy-start.1) | copy-done | bytes 36888
  2.9 0.0 copy-start.2
  2.9 0.8 %copy-done.2 = f32[1,3,24,128]{3,2,1,0:T(8,128)S(1)} copy-done((f32[1,3,24,128]{3,2,1,0:T(8,128)S(1)}, f32[1,3,24,128]{3,2,1,0:T(8,128)}, u32[]{:S(2)}) %copy-start.2) | copy-done | bytes 36888
  3.6 0.0 copy-start.3
  3.6 0.8 %copy-done.3 = f32[1,3,24,128]{3,2,1,0:T(8,128)S(1)} copy-done((f32[1,3,24,128]{3,2,1,0:T(8,128)S(1)}, f32[1,3,24,128]{3,2,1,0:T(8,128)}, u32[]{:S(2)}) %copy-start.3) | copy-done | bytes 36888
  4.4 0.0 copy-start.4
  4.4 0.7 %copy-done.4 = s32[24,26]{1,0:T(8,128)S(1)} copy-done((s32[24,26]{1,0:T(8,128)S(1)}, s32[24,26]{1,0:T(8,128)}, u32[]{:S(2)}) %copy-start.4) | copy-done | bytes 2520
  5.1 0.0 copy-start.5
  5.1 0.7 %copy-done.5 = f32[24,128]{1,0:T(8,128)S(1)} copy-done((f32[24,128]{1,0:T(8,128)S(1)}, f32[24,128]{1,0:T(8,128)}, u32[]{:S(2)}) %copy-start.5) | copy-done | bytes 12312
  5.8 0.0 copy-start.6
  5.8 0.7 %copy-done.6 = f32[24,128]{1,0:T(8,128)S(1)} copy-done((f32[24,128]{1,0:T(8,128)S(1)}, f32[24,128]{1,0:T(8,128)}, u32[]{:S(2)}) %copy-start.6) | copy-done | bytes 12312
  6.5 26.2 %shard_map.112 = (f32[3,24,128]{2,1,0:T(8,128)S(1)}, f32[3,24,128]{2,1,0:T(8,128)S(1)}, f32[3,24,128]{2,1,0:T(8,128)S(1)}) custom-call(f32[2,4,4]{2,1,0:T(4,128)S(1)} %copy-done.7, s32[96]{0:T(128)S(1)} %copy-done.8, s32[24,26]{1,0:T(8,128)S(1)} %copy-done.4, f32[3,24,128]{2,1,0:T(8,128)S(1)} %bitcast.10, f32[3,24,128]{2,1,0:T(8,128)S(1)} %bitcast.11, ...), custom_call_target="tpu_custom_call" | custom-call | tf_op jit(solution)/shard_map/pallas_call | solution.py:349
  32.8 0.6 %copy.15 = f32[1,3,24,128]{3,2,1,0:T(8,128)} copy(f32[1,3,24,128]{3,2,1,0:T(8,128)S(1)} %bitcast.9) | data formatting | bytes 73728
  33.4 0.6 %copy.16 = f32[1,3,24,128]{3,2,1,0:T(8,128)} copy(f32[1,3,24,128]{3,2,1,0:T(8,128)S(1)} %bitcast.8) | data formatting | bytes 73728
  34.0 0.6 %copy.17 = f32[1,3,24,128]{3,2,1,0:T(8,128)} copy(f32[1,3,24,128]{3,2,1,0:T(8,128)S(1)} %bitcast.7) | data formatting | bytes 73728
Async XLA Ops:
  0.6 0.7 %copy-start.7 = (f32[2,4,4]{2,1,0:T(4,128)S(1)}, f32[2,4,4]{2,1,0:T(4,128)}, u32[]{:S(2)}) copy-start(f32[2,4,4]{2,1,0:T(4,128)} %constant.2.clone.kicks_ref) | copy-start | bytes 388
  0.6 0.7 %copy-start.8 = (s32[96]{0:T(128)S(1)}, s32[96]{0:T(128)}, u32[]{:S(2)}) copy-start(s32[96]{0:T(128)} %counts_ref.1) | copy-start | bytes 1156
  1.3 0.8 %copy-start = (f32[1,3,24,128]{3,2,1,0:T(8,128)S(1)}, f32[1,3,24,128]{3,2,1,0:T(8,128)}, u32[]{:S(2)}) copy-start(f32[1,3,24,128]{3,2,1,0:T(8,128)} %param.9) | copy-start | bytes 110596
  2.1 0.8 %copy-start.1 = (f32[1,3,24,128]{3,2,1,0:T(8,128)S(1)}, f32[1,3,24,128]{3,2,1,0:T(8,128)}, u32[]{:S(2)}) copy-start(f32[1,3,24,128]{3,2,1,0:T(8,128)} %param.10) | copy-start | bytes 110596
  2.9 0.8 %copy-start.2 = (f32[1,3,24,128]{3,2,1,0:T(8,128)S(1)}, f32[1,3,24,128]{3,2,1,0:T(8,128)}, u32[]{:S(2)}) copy-start(f32[1,3,24,128]{3,2,1,0:T(8,128)} %param.11) | copy-start | bytes 110596
  3.6 0.8 %copy-start.3 = (f32[1,3,24,128]{3,2,1,0:T(8,128)S(1)}, f32[1,3,24,128]{3,2,1,0:T(8,128)}, u32[]{:S(2)}) copy-start(f32[1,3,24,128]{3,2,1,0:T(8,128)} %param.12) | copy-start | bytes 110596
  4.4 0.7 %copy-start.4 = (s32[24,26]{1,0:T(8,128)S(1)}, s32[24,26]{1,0:T(8,128)}, u32[]{:S(2)}) copy-start(s32[24,26]{1,0:T(8,128)} %list_ref.1) | copy-start | bytes 7492
  5.1 0.7 %copy-start.5 = (f32[24,128]{1,0:T(8,128)S(1)}, f32[24,128]{1,0:T(8,128)}, u32[]{:S(2)}) copy-start(f32[24,128]{1,0:T(8,128)} %mass_ref.1) | copy-start | bytes 36868
  5.8 0.7 %copy-start.6 = (f32[24,128]{1,0:T(8,128)S(1)}, f32[24,128]{1,0:T(8,128)}, u32[]{:S(2)}) copy-start(f32[24,128]{1,0:T(8,128)} %str_ref.1) | copy-start | bytes 36868

commit v6 on v5

--- a/solution.py
+++ b/solution.py
@@ -310,7 +310,7 @@
         rows_f[c] = (PAIR_SCALE / ROOT) * weight * (own * sums[3:4] - sums)
         return carry
 
-    lax.fori_loop(0, cells, one_cell, 0, unroll=4)
+    lax.fori_loop(0, cells, one_cell, 0, unroll=8)
 
     for copy in copies_p:
         copy.wait_recv()

time: 35.2 us -> 34.4 us (0.977)
  Pallas kernels: 26.2 us -> 25.5 us
    pallas_call x1, Pallas kernels: 26.2 us -> 25.5 us  [per_device(): pl.pallas_call(functools.partial(kernel, beads, spaces, coef), out_shape=...]
where the time goes in v6:
time: 34.4 us; the launch traced here: 33.9 us
  Pallas kernels  25.5 us (74%)
  local copies, waits for them, and re-layouts  7.72 us (22%)
  between operations  0.67 us (2%)
    pallas_call x1, Pallas kernels, per_device(): pl.pallas_call(functools.partial(kernel, beads, spaces, coef), out_shape=...  25.5 us
    unnamed x21, local copies, waits for them, and re-layouts  7.72 us

profile of v6, /device:TPU:1, one launch (start us, length us, event | category | flops | bytes accessed | tf_op | source)
XLA Modules:
  0.0 33.9 jit_solution(11187030982567362802)
XLA Ops:
  0.6 0.0 copy-start.7
  0.6 0.0 copy-start.8
  0.7 0.7 %copy-done.7 = f32[2,4,4]{2,1,0:T(4,128)S(1)} copy-done((f32[2,4,4]{2,1,0:T(4,128)S(1)}, f32[2,4,4]{2,1,0:T(4,128)}, u32[]{:S(2)}) %copy-start.7) | copy-done | bytes 152
  1.3 0.0 copy-done.8
  1.3 0.0 copy-start
  1.3 0.8 %copy-done = f32[1,3,24,128]{3,2,1,0:T(8,128)S(1)} copy-done((f32[1,3,24,128]{3,2,1,0:T(8,128)S(1)}, f32[1,3,24,128]{3,2,1,0:T(8,128)}, u32[]{:S(2)}) %copy-start) | copy-done | bytes 36888
  2.1 0.0 copy-start.1
  2.1 0.8 %copy-done.1 = f32[1,3,24,128]{3,2,1,0:T(8,128)S(1)} copy-done((f32[1,3,24,128]{3,2,1,0:T(8,128)S(1)}, f32[1,3,24,128]{3,2,1,0:T(8,128)}, u32[]{:S(2)}) %copy-start.1) | copy-done | bytes 36888
  2.9 0.0 copy-start.2
  2.9 0.8 %copy-done.2 = f32[1,3,24,128]{3,2,1,0:T(8,128)S(1)} copy-done((f32[1,3,24,128]{3,2,1,0:T(8,128)S(1)}, f32[1,3,24,128]{3,2,1,0:T(8,128)}, u32[]{:S(2)}) %copy-start.2) | copy-done | bytes 36888
  3.6 0.0 copy-start.3
  3.6 0.8 %copy-done.3 = f32[1,3,24,128]{3,2,1,0:T(8,128)S(1)} copy-done((f32[1,3,24,128]{3,2,1,0:T(8,128)S(1)}, f32[1,3,24,128]{3,2,1,0:T(8,128)}, u32[]{:S(2)}) %copy-start.3) | copy-done | bytes 36888
  4.4 0.0 copy-start.4
  4.4 0.7 %copy-done.4 = s32[24,26]{1,0:T(8,128)S(1)} copy-done((s32[24,26]{1,0:T(8,128)S(1)}, s32[24,26]{1,0:T(8,128)}, u32[]{:S(2)}) %copy-start.4) | copy-done | bytes 2520
  5.1 0.0 copy-start.5
  5.1 0.7 %copy-done.5 = f32[24,128]{1,0:T(8,128)S(1)} copy-done((f32[24,128]{1,0:T(8,128)S(1)}, f32[24,128]{1,0:T(8,128)}, u32[]{:S(2)}) %copy-start.5) | copy-done | bytes 12312
  5.8 0.0 copy-start.6
  5.8 0.7 %copy-done.6 = f32[24,128]{1,0:T(8,128)S(1)} copy-done((f32[24,128]{1,0:T(8,128)S(1)}, f32[24,128]{1,0:T(8,128)}, u32[]{:S(2)}) %copy-start.6) | copy-done | bytes 12312
  6.5 25.5 %shard_map.112 = (f32[3,24,128]{2,1,0:T(8,128)S(1)}, f32[3,24,128]{2,1,0:T(8,128)S(1)}, f32[3,24,128]{2,1,0:T(8,128)S(1)}) custom-call(f32[2,4,4]{2,1,0:T(4,128)S(1)} %copy-done.7, s32[96]{0:T(128)S(1)} %copy-done.8, s32[24,26]{1,0:T(8,128)S(1)} %copy-done.4, f32[3,24,128]{2,1,0:T(8,128)S(1)} %bitcast.10, f32[3,24,128]{2,1,0:T(8,128)S(1)} %bitcast.11, ...), custom_call_target="tpu_custom_call" | custom-call | tf_op jit(solution)/shard_map/pallas_call | solution.py:349
  32.0 0.6 %copy.15 = f32[1,3,24,128]{3,2,1,0:T(8,128)} copy(f32[1,3,24,128]{3,2,1,0:T(8,128)S(1)} %bitcast.9) | data formatting | bytes 73728
  32.6 0.6 %copy.16 = f32[1,3,24,128]{3,2,1,0:T(8,128)} copy(f32[1,3,24,128]{3,2,1,0:T(8,128)S(1)} %bitcast.8) | data formatting | bytes 73728
  33.3 0.6 %copy.17 = f32[1,3,24,128]{3,2,1,0:T(8,128)} copy(f32[1,3,24,128]{3,2,1,0:T(8,128)S(1)} %bitcast.7) | data formatting | bytes 73728
Async XLA Ops:
  0.6 0.7 %copy-start.7 = (f32[2,4,4]{2,1,0:T(4,128)S(1)}, f32[2,4,4]{2,1,0:T(4,128)}, u32[]{:S(2)}) copy-start(f32[2,4,4]{2,1,0:T(4,128)} %constant.2.clone.kicks_ref) | copy-start | bytes 388
  0.6 0.7 %copy-start.8 = (s32[96]{0:T(128)S(1)}, s32[96]{0:T(128)}, u32[]{:S(2)}) copy-start(s32[96]{0:T(128)} %counts_ref.1) | copy-start | bytes 1156
  1.3 0.8 %copy-start = (f32[1,3,24,128]{3,2,1,0:T(8,128)S(1)}, f32[1,3,24,128]{3,2,1,0:T(8,128)}, u32[]{:S(2)}) copy-start(f32[1,3,24,128]{3,2,1,0:T(8,128)} %param.9) | copy-start | bytes 110596
  2.1 0.8 %copy-start.1 = (f32[1,3,24,128]{3,2,1,0:T(8,128)S(1)}, f32[1,3,24,128]{3,2,1,0:T(8,128)}, u32[]{:S(2)}) copy-start(f32[1,3,24,128]{3,2,1,0:T(8,128)} %param.10) | copy-start | bytes 110596
  2.9 0.8 %copy-start.2 = (f32[1,3,24,128]{3,2,1,0:T(8,128)S(1)}, f32[1,3,24,128]{3,2,1,0:T(8,128)}, u32[]{:S(2)}) copy-start(f32[1,3,24,128]{3,2,1,0:T(8,128)} %param.11) | copy-start | bytes 110596
  3.6 0.8 %copy-start.3 = (f32[1,3,24,128]{3,2,1,0:T(8,128)S(1)}, f32[1,3,24,128]{3,2,1,0:T(8,128)}, u32[]{:S(2)}) copy-start(f32[1,3,24,128]{3,2,1,0:T(8,128)} %param.12) | copy-start | bytes 110596
  4.4 0.7 %copy-start.4 = (s32[24,26]{1,0:T(8,128)S(1)}, s32[24,26]{1,0:T(8,128)}, u32[]{:S(2)}) copy-start(s32[24,26]{1,0:T(8,128)} %list_ref.1) | copy-start | bytes 7492
  5.1 0.7 %copy-start.5 = (f32[24,128]{1,0:T(8,128)S(1)}, f32[24,128]{1,0:T(8,128)}, u32[]{:S(2)}) copy-start(f32[24,128]{1,0:T(8,128)} %mass_ref.1) | copy-start | bytes 36868
  5.8 0.7 %copy-start.6 = (f32[24,128]{1,0:T(8,128)S(1)}, f32[24,128]{1,0:T(8,128)}, u32[]{:S(2)}) copy-start(f32[24,128]{1,0:T(8,128)} %str_ref.1) | copy-start | bytes 36868
